TPU v7x, 512 devices: a whole 4x4x16 slice. The times are simulated.
512 devices in a mesh: mem: 16 (over z), slab: 32 (over y, x, core).
Axes of the slice: x: 4, y: 4, z: 16, core: 2. Of those that a mesh axis runs over, the one named last changes fastest.
Arguments:
- ensemble: float32 [256, 4096, 128], P('mem', 'slab'), may hold values from -6 to 6
- diffusivity: float32 [4096, 128], P('slab'), may hold values from 0.15 to 0.25
- velocity: float32 [2, 4096, 128], P(None, 'slab'), may hold values from -0.5 to 0.5
- obs_value: float32 [655360], P(('mem', 'slab')), may hold values from -6 to 6
- obs_weight: float32 [655360], P(('mem', 'slab')), may hold values from 0.3 to 12
- obs_slab: int32 [655360, 1], P(('mem', 'slab')), may hold values from 0 to 31; in each aligned block of 1280 rows (0 to 1279, 1280 to 2559, ...) at most 80 rows name the same one
- obs_cell: int32 [655360], P(('mem', 'slab')), may hold values from 0 to 1023
Outputs:
- analysis: float32 [256, 4096, 128], P('mem', 'slab')
Inputs may be any that keep to these rules, and one draw needn't show every extreme that they name: `obs_slab`: among the 1280 observations stored on one device, no slab is named more than 80 times; on some device one slab is named exactly 80 times.
All inputs are finite; a program needn't handle non-finite values.
Results may differ from a plain program's by a relative error of at most 0.0085.
Values sent between devices are 32-bit elements; how exact they have to be, the bound alone decides.
A program may use at most 128 MiB of HBM per device.

v0:
```python
import jax
import jax.numpy as jnp
from jax import lax
from jax.sharding import PartitionSpec as P

STEPS = 4
NS_STEPS = 5


def padded_2(shard, sides, width):
    for axis, dim in sides:
        peers, length = (lax.axis_size(axis), shard.shape[dim])
        up = [(i, (i + 1) % peers) for i in range(peers)]
        down = [(j, i) for i, j in up]
        last = lax.slice_in_dim(shard, length - width, length, axis=dim)
        leading = lax.slice_in_dim(shard, 0, width, axis=dim)
        before = lax.ppermute(last, axis, up)
        after = lax.ppermute(leading, axis, down)
        shard = jnp.concatenate([before, shard, after], axis=dim)
    return shard


def stencil(center, upper_row, lower_row, diffuse, drift_x, drift_y):
    east_side = jnp.roll(center, -1, axis=-1)
    west_side = jnp.roll(center, 1, axis=-1)
    laplace = east_side + west_side + upper_row + lower_row - 4.0 * center
    return (
        center
        + diffuse * laplace
        - 0.5 * drift_x * (east_side - west_side)
        - 0.5 * drift_y * (lower_row - upper_row)
    )


def analyse(fields, obs_vals, obs_wts, obs_cells):
    members, patches, width = fields.shape
    center_mean = jnp.mean(fields, axis=0)
    spread = (fields - center_mean[None]).astype(jnp.bfloat16)
    flat_mean = center_mean.reshape(-1)
    at_obs = jnp.take(spread.reshape(members, -1), obs_cells, axis=1)
    misfit = obs_vals - jnp.take(flat_mean, obs_cells)
    patch_of = obs_cells // width
    weights = obs_wts[None, :] * (
        patch_of[None, :] == jnp.arange(patches, dtype=jnp.int32)[:, None]
    ).astype(jnp.float32)

    def patch_gram(patch_weights):
        weighted = (at_obs * patch_weights[None, :]).astype(jnp.bfloat16)
        return jnp.einsum("mo,no->mn", weighted, at_obs, preferred_element_type=jnp.float32)

    gram = lax.map(patch_gram, weights)
    eye_f = jnp.eye(members, dtype=jnp.float32)
    system = (members - 1) * eye_f[None] + gram
    scale = 8.0 * jnp.sqrt(jnp.sum(system * system, axis=(1, 2)) / members)
    iterate = (system / scale[:, None, None]).astype(jnp.bfloat16)
    inverse_root = jnp.broadcast_to(eye_f.astype(jnp.bfloat16), iterate.shape)
    for sweep in range(NS_STEPS):
        product = jnp.einsum(
            "pij,pjk->pik", inverse_root, iterate, preferred_element_type=jnp.float32
        )
        factor = (1.5 * eye_f[None] - 0.5 * product).astype(jnp.bfloat16)
        iterate = jnp.einsum(
            "pij,pjk->pik", iterate, factor, preferred_element_type=jnp.float32
        ).astype(jnp.bfloat16)
        inverse_root = jnp.einsum(
            "pij,pjk->pik", factor, inverse_root, preferred_element_type=jnp.float32
        ).astype(jnp.bfloat16)
    root_f = inverse_root.astype(jnp.float32)
    pull = jnp.dot(
        at_obs.astype(jnp.float32), (weights * misfit[None, :]).T, precision=lax.Precision.HIGHEST
    )
    first = jnp.einsum("pij,jp->pi", root_f, pull, precision=lax.Precision.HIGHEST)
    mean_gain = (
        jnp.einsum("pij,pj->pi", root_f, first, precision=lax.Precision.HIGHEST) / scale[:, None]
    )
    transform = (
        jnp.sqrt((members - 1) / scale)[:, None, None] * root_f + mean_gain[:, None, :]
    ).astype(jnp.bfloat16)
    update = jnp.einsum("pik,kpx->ipx", transform, spread, preferred_element_type=jnp.float32)
    return center_mean[None] + update


def shards(ensemble, diffusivity, velocity, obs_value, obs_weight, obs_slab, obs_cell):
    n_slab = lax.axis_size("slab")
    local_members = ensemble.shape[0]
    rows = ensemble.shape[1]
    stacked = jnp.concatenate([ensemble, diffusivity[None], velocity], axis=0)
    padded = padded_2(stacked, (("slab", 1),), STEPS)
    fields = padded[:local_members]
    coeffs = padded[local_members:]
    length = rows + 2 * STEPS
    for step in range(STEPS):
        low_row = step + 1
        high_row = length - step - 1
        fields = stencil(
            fields[:, 1:-1],
            fields[:, :-2],
            fields[:, 2:],
            coeffs[0, low_row:high_row],
            coeffs[1, low_row:high_row],
            coeffs[2, low_row:high_row],
        )
    patch_fields = lax.all_to_all(fields, "mem", split_axis=1, concat_axis=0, tiled=True)
    obs_dev = obs_value.shape[0]
    capacity = max(2, 2 * obs_dev // n_slab)
    target = obs_slab[:, 0]
    choose = (target[:, None] == jnp.arange(n_slab, dtype=jnp.int32)[None, :]).astype(jnp.int32)
    before = jnp.cumsum(choose, axis=0) - choose
    rank_in = jnp.sum(before * choose, axis=1)
    slot = target * capacity + rank_in
    records = jnp.stack([obs_value, obs_weight, obs_cell.astype(jnp.float32)])
    outgoing = (
        jnp.zeros((3, n_slab * capacity), jnp.float32)
        .at[:, slot]
        .set(records)
        .reshape(3, n_slab, capacity)
    )
    buffer = lax.all_to_all(outgoing, "slab", split_axis=1, concat_axis=1, tiled=True).reshape(
        3, n_slab * capacity
    )
    analysed = analyse(patch_fields, buffer[0], buffer[1], buffer[2].astype(jnp.int32))
    return lax.all_to_all(analysed, "mem", split_axis=0, concat_axis=1, tiled=True)


def solution(mesh):
    return jax.shard_map(
        shards,
        mesh=mesh,
        in_specs=(
            P("mem", "slab", None),
            P("slab", None),
            P(None, "slab", None),
            P(("mem", "slab")),
            P(("mem", "slab")),
            P(("mem", "slab"), None),
            P(("mem", "slab")),
        ),
        out_specs=P("mem", "slab", None),
        check_vma=False,
    )
```

profile of v0, /device:TPU:2, one launch (start us, length us, event | category | flops | bytes accessed | tf_op | source)
XLA Modules:
  0.0 227.1 jit_solution(4383249677333947876)
XLA Ops:
  0.0 1.9 copy.30
  2.0 1.9 collective-permute-start
  4.0 3.6 %collective-permute-start.1 = (f32[19,4,128]{2,0,1:T(8,128)S(1)}, f32[19,4,128]{2,0,1:T(8,128)S(1)}, u32[]{:S(2)}, u32[]{:S(2)}) collective-permute-start(f32[19,4,128]{2,0,1:T(8,128)S(1)} %get-tuple-element.70), channel_id=1, source_target_pairs={{1,0},{2,1},{3,2},{4,3},{5,4},{6,5},{7,6},{8,7},{9,8},{10,9},{11,1... | collective-permute-start | bytes 116744 | tf_op jit(solution)/shard_map/ppermute | solution.py:18
  7.7 9.1 %reduce-window.6 = s32[32,10,128]{2,1,0:T(8,128)S(1)} reduce-window(s32[32,10,128]{2,1,0:T(8,128)S(1)} %fusion.16, s32[]{:T(128)} %copy.96), window={size=1x1x128 pad=0_0x0_0x127_0}, to_apply=%region_1.2 | reduce-window | flops 5201920 | bytes 327684 | tf_op jit(solution)/shard_map/reduce-window
  17.9 6.4 %scatter_custom_fusion = f32[3,2560]{0,1:T(8,128)S(1)} fusion(s32[1280]{0:T(1024)S(1)} %fusion.31, f32[1280,3]{1,0:T(8,128)S(1)} %copy.36, f32[]{:T(128)} %constant.42.clone.1), kind=kCustom, calls=%fused_computation.51 | custom fusion | bytes 30724 | tf_op jit(solution)/shard_map/scatter | solution.py:115
  24.7 0.8 reshape.192
  25.5 12.7 %all-to-all-start.1 = ((f32[32,1,240]{2,1,0:T(1,128)}), f32[32,1,240]{2,1,0:T(1,128)S(1)}, u32[]{:S(2)}, u32[]{:S(2)}) async-start(f32[32,1,240]{2,1,0:T(1,128)} %reshape.192), calls=%async_computation.1 | async-start | bytes 65536 | tf_op jit(solution)/shard_map/all_to_all | solution.py:118
  39.5 1.0 multiply_subtract_fusion
  41.6 1.0 multiply_subtract_fusion.1
  43.6 1.0 multiply_subtract_fusion.2
  45.3 1.9 multiply_subtract_fusion.3
  47.2 10.1 %all-to-all-start = ((f32[16,128,128]{2,0,1:T(8,128)}), f32[16,128,128]{2,0,1:T(8,128)S(1)}, u32[]{:S(2)}, u32[]{:S(2)}) async-start(f32[16,128,128]{2,0,1:T(8,128)} %multiply_subtract_fusion.3), calls=%async_computation | async-start | bytes 2097152 | tf_op jit(solution)/shard_map/all_to_all | solution.py:103
  57.3 0.7 convert_convert_fusion
  58.0 0.7 fusion.14
  58.7 0.5 broadcast.269
  59.2 0.7 reduce.23
  60.2 0.7 squeeze.3
  61.2 46.3 %all-to-all-done = f32[16,128,128]{2,0,1:T(8,128)S(1)} async-done(((f32[16,128,128]{2,0,1:T(8,128)}), f32[16,128,128]{2,0,1:T(8,128)S(1)}, u32[]{:S(2)}, u32[]{:S(2)}) %all-to-all-start) | async-done | bytes 1048608 | tf_op jit(solution)/shard_map/all_to_all | solution.py:103
  108.1 0.6 broadcast_multiply_fusion
  109.2 9.4 %gather_fusion.1 = f32[2560]{0:T(1024)S(1)} fusion(f32[1024]{0:T(1024)S(1)} %get-tuple-element.87, s32[3072]{0:T(1024)S(1)} %pad_clamp_fusion), kind=kCustom, calls=%fused_computation.1 | custom fusion | bytes 30720 | tf_op jit(solution)/shard_map/jit(_take)/gather | solution.py:41
  118.9 7.6 %gather_fusion = bf16[2560,256]{1,0:T(8,128)(2,1)S(1)} fusion(bf16[256,1024]{0,1:T(8,128)(2,1)S(1)} %subtract_convert_fusion.5, s32[3072]{0:T(1024)S(1)} %pad_clamp_fusion), kind=kCustom, calls=%fused_computation | custom fusion | bytes 2631680 | tf_op jit(solution)/shard_map/jit(_take)/gather | solution.py:40
  126.5 0.7 select_subtract_fusion
  127.5 2.2 fusion.10
  129.7 2.6 %copy.40 = bf16[256,2560]{1,0:T(8,128)(2,1)} copy(bf16[256,2560]{0,1:T(8,128)(2,1)} %fusion.10) | data formatting | bytes 2621440 | tf_op jit(solution)/shard_map/while | solution.py:51
  132.3 18.6 %while.10 = (s32[]{:T(128)}, f32[8,256,256]{2,1,0:T(8,128)S(1)}, bf16[256,2560]{1,0:T(8,128)(2,1)}, f32[8,2560]{1,0:T(8,128)S(1)}, s32[]{:T(128)}) while((s32[]{:T(128)}, f32[8,256,256]{2,1,0:T(8,128)S(1)}, bf16[256,2560]{1,0:T(8,128)(2,1)}, f32[8,2560]{1,0:T(8,128)S(1)}, s32[]{:T(128)}) %tuple.49), condition=%wide.region_6.7_spmd, body=%wide.region_5.6_spmd.sunk | while | flops 337510400 | bytes 2916929 | solution.py:51
  132.3 2.3 fusion.75
  134.6 2.3 fusion.75
  137.0 2.3 fusion.75
  139.3 2.3 fusion.75
  141.6 2.3 fusion.75
  144.0 2.3 fusion.75
  146.3 2.3 fusion.75
  148.6 2.3 fusion.75
  151.3 0.6 divide_convert_fusion
  153.6 0.4 subtract_convert_fusion.3
  155.0 0.4 subtract_convert_fusion.2
  156.6 0.8 fusion.5
  157.8 0.9 convolution_bitcast_fusion
  158.7 0.5 subtract_convert_fusion.1
  159.2 0.4 convolution_convert_fusion.2
  159.6 0.5 copy-done.8
  160.1 1.7 subtract_convert_fusion
  161.8 1.7 convolution_convert_fusion
  163.5 0.9 fusion.29
  164.4 0.9 fusion.27
  165.4 0.6 fusion.4
  166.5 59.5 %all_to_all.44 = f32[256,8,128]{2,1,0:T(8,128)S(1)} all-to-all(f32[256,8,128]{2,1,0:T(8,128)S(1)} %copy.42), channel_id=1, replica_groups=mesh['mem'=16,'slab'=32] {'mem'}, dimensions={0} | all-to-all | bytes 2097152 | tf_op jit(solution)/shard_map/all_to_all | solution.py:122
  226.0 1.1 copy.83
  (108 shorter events, 13.1 us)
Async XLA Ops:
  0.0 1.9 copy-start.6
  0.0 2.0 copy-start.3
  1.9 5.7 %copy-start.10 = (s32[1280,1]{0,1:T(1,128)S(1)}, s32[1280,1]{0,1:T(1,128)}, u32[]{:S(2)}) copy-start(s32[1280,1]{0,1:T(1,128)} %param.14) | copy-start | bytes 15364
  2.0 36.2 %collective-permute-start = (f32[19,4,128]{2,0,1:T(8,128)S(1)}, f32[19,4,128]{2,0,1:T(8,128)S(1)}, u32[]{:S(2)}, u32[]{:S(2)}) collective-permute-start(f32[19,4,128]{2,0,1:T(8,128)S(1)} %get-tuple-element.69), channel_id=1, source_target_pairs={{0,1},{1,2},{2,3},{3,4},{4,5},{5,6},{6,7},{7,8},{8,9},{9,10},{10,1... | collective-permute-start | bytes 116744 | tf_op jit(solution)/shard_map/ppermute | solution.py:17
  4.0 34.3 %collective-permute-start.1 = (f32[19,4,128]{2,0,1:T(8,128)S(1)}, f32[19,4,128]{2,0,1:T(8,128)S(1)}, u32[]{:S(2)}, u32[]{:S(2)}) collective-permute-start(f32[19,4,128]{2,0,1:T(8,128)S(1)} %get-tuple-element.70), channel_id=1, source_target_pairs={{1,0},{2,1},{3,2},{4,3},{5,4},{6,5},{7,6},{8,7},{9,8},{10,9},{11,1... | collective-permute-start | bytes 116744 | tf_op jit(solution)/shard_map/ppermute | solution.py:18
  7.7 9.8 %copy-start.13 = (s32[1280]{0:T(1024)S(1)}, s32[1280]{0:T(1024)}, u32[]{:S(2)}) copy-start(s32[1280]{0:T(1024)} %param.15) | copy-start | bytes 15364
  7.7 9.8 %copy-start.14 = (f32[1280]{0:T(1024)S(1)}, f32[1280]{0:T(1024)}, u32[]{:S(2)}) copy-start(f32[1280]{0:T(1024)} %param.12) | copy-start | bytes 15364
  7.7 9.8 %copy-start.15 = (f32[1280]{0:T(1024)S(1)}, f32[1280]{0:T(1024)}, u32[]{:S(2)}) copy-start(f32[1280]{0:T(1024)} %param.13) | copy-start | bytes 15364
  25.5 21.7 %all-to-all-start.1 = ((f32[32,1,240]{2,1,0:T(1,128)}), f32[32,1,240]{2,1,0:T(1,128)S(1)}, u32[]{:S(2)}, u32[]{:S(2)}) async-start(f32[32,1,240]{2,1,0:T(1,128)} %reshape.192), calls=%async_computation.1 | async-start | bytes 65536 | tf_op jit(solution)/shard_map/all_to_all | solution.py:118
  47.2 60.3 %all-to-all-start = ((f32[16,128,128]{2,0,1:T(8,128)}), f32[16,128,128]{2,0,1:T(8,128)S(1)}, u32[]{:S(2)}, u32[]{:S(2)}) async-start(f32[16,128,128]{2,0,1:T(8,128)} %multiply_subtract_fusion.3), calls=%async_computation | async-start | bytes 2097152 | tf_op jit(solution)/shard_map/all_to_all | solution.py:103
  118.8 7.6 %copy-start.9 = (f32[2560]{0:T(1024)S(1)}, f32[2560]{0:T(1024)}, u32[]{:S(2)}) copy-start(f32[2560]{0:T(1024)} %squeeze.3) | copy-start | bytes 30724
  126.4 1.1 copy-start.1
  129.7 2.6 %copy-start = (f32[8,256,256]{2,1,0:T(8,128)S(1)}, f32[8,256,256]{2,1,0:T(8,128)}, u32[]{:S(2)}) copy-start(f32[8,256,256]{2,1,0:T(8,128)} %custom-call.4) | copy-start | bytes 6291460
  151.2 0.9 copy-start.5
  151.3 1.0 copy-start.7
  155.9 0.7 copy-start.11
  156.3 1.5 copy-start.2
  156.3 1.5 copy-start.12
  159.2 1.0 copy-start.8
  163.5 1.9 copy-start.4
where the time goes:
time: 228 us; the launch traced here: 227 us
  blocking collectives  59.5 us (26%)
  waiting for transfers between devices  46.3 us (20%)
  local copies, waits for them, and re-layouts  38.8 us (17%)
  matrix products  29.6 us (13%)
  starting transfers between devices  28.4 us (12%)
  other arithmetic  23.6 us (10%)
    all_to_all x1, blocking collectives, shards(): lax.all_to_all(analysed, 'mem', split_axis=0, concat_axis=1, tiled=True)  59.5 us
    all_to_all x1, waiting for transfers between devices, shards(): lax.all_to_all(fields, 'mem', split_axis=1, concat_axis=0, tiled=True)  46.3 us
    dot_general x8, matrix products, patch_gram(): jnp.einsum('mo,no->mn', weighted, at_obs, preferred_element_type=jnp.floa...  18.1 us
    all_to_all x1, starting transfers between devices, shards(): lax.all_to_all(outgoing, 'slab', split_axis=1, concat_axis=1, tiled=True)  12.7 us
    all_to_all x1, starting transfers between devices, shards(): lax.all_to_all(fields, 'mem', split_axis=1, concat_axis=0, tiled=True)  10.1 us
    gather x1, local copies, waits for them, and re-layouts, analyse(): misfit = obs_vals - jnp.take(flat_mean, obs_cells)  9.39 us
    another operation x3, other arithmetic  9.24 us
    gather x1, local copies, waits for them, and re-layouts, analyse(): at_obs = jnp.take(spread.reshape(members, -1), obs_cells, axis=1)  7.57 us
  transfers between devices with their start and end apart: 4, of which 1 were waited for; matrix products, arithmetic and copies ran while one was open for 13% of the time, Pallas kernels for 0%

commit v1 on v0

v1 whole, which is shorter than its diff:
```python
import jax
import jax.numpy as jnp
from jax import lax
from jax.experimental import pallas as pl
from jax.experimental.pallas import tpu as pltpu
from jax.sharding import PartitionSpec as P

STEPS = 4
NS_STEPS = 5
NM = 16
NS = 32
K = 8
M = 256
ML = 16
W = 128
OBS = 1280
MESH = pl.DeviceIdType.MESH
F32 = jnp.float32
BF16 = jnp.bfloat16
ORDER = (8, 7, 9, 6, 10, 5, 11, 4, 12, 3, 13, 2, 14, 1, 15)


def dot(a, b, dims):
    return lax.dot_general(a, b, (dims, ((), ())), preferred_element_type=F32)


def nn(a, b):
    return dot(a, b, ((1,), (0,)))


def nt(a, b):
    return dot(a, b, ((1,), (1,)))


def parts(x):
    hi = x.astype(BF16).astype(F32)
    rest = x - hi
    mid = rest.astype(BF16).astype(F32)
    return hi, mid, rest - mid


def row_times(row, mat_t):
    hi, mid, lo = parts(row)
    n = row.shape[1]
    at = lax.broadcasted_iota(jnp.int32, (16, n), 0)
    stack = jnp.where(at == 0, hi, jnp.where(at == 1, mid, jnp.where(at == 2, lo, 0.0)))
    return jnp.sum(nt(stack.astype(BF16), mat_t), axis=0, keepdims=True)


def advance(x, coeffs):
    rows = x.shape[0]
    for _ in range(STEPS):
        x = (
            coeffs[0] * x
            + coeffs[1] * pltpu.roll(x, W - 1, 1)
            + coeffs[2] * pltpu.roll(x, 1, 1)
            + coeffs[3] * pltpu.roll(x, 1, 0)
            + coeffs[4] * pltpu.roll(x, rows - 1, 0)
        )
    return x


def combine(d, vx, vy):
    ax, ay = 0.5 * vx, 0.5 * vy
    return 1.0 - 4.0 * d, d - ax, d + ax, d + ay, d - ay


def kernel(
    ens_ref, dif_ref, vel_ref, val_ref, wt_ref, slab_ref, cell_ref, out_ref,
    ens, cf, cfe, hs, hr, send, recv, ana, ret, tab, orx, wtot, utot,
    ens_sem, hs_sem, hr_sem, fs_sem, fr_sem, rs_sem, rr_sem, os_sem, or_sem,
):
    me = lax.axis_index("mem")
    sl = lax.axis_index("slab")

    def mem_peer(d):
        return lax.rem(me + d, NM)

    load = pltpu.make_async_copy(ens_ref, ens, ens_sem)
    load.start()
    bar = pltpu.get_barrier_semaphore()

    @pl.loop(1, NM)
    def _(d):
        pl.semaphore_signal(bar, inc=1, device_id={"mem": mem_peer(d)}, device_id_type=MESH)

    @pl.loop(1, NS)
    def _(d):
        pl.semaphore_signal(
            bar, inc=1, device_id={"slab": lax.rem(sl + d, NS)}, device_id_type=MESH
        )

    dif, vx, vy = dif_ref[...], vel_ref[0], vel_ref[1]
    for i, c in enumerate(combine(dif, vx, vy)):
        cf[i] = c
    hs[0, 16], hs[1, 16] = dif[0:8], dif[120:128]
    hs[0, 17], hs[1, 17] = vx[0:8], vx[120:128]
    hs[0, 18], hs[1, 18] = vy[0:8], vy[120:128]
    load.wait()

    @pl.loop(0, ML)
    def _(m):
        x = ens[m]
        hs[0, m] = x[0:8]
        hs[1, m] = x[120:128]

    @pl.loop(0, ML)
    def _(m):
        x = advance(ens[m], cf)
        for q in range(1, NM - 1):
            send[q, pl.ds(m, K, stride=ML), :] = x[q * 8 : q * 8 + 8]

    pl.semaphore_wait(bar, NM - 1 + NS - 1)

    up = lax.rem(sl + NS - 1, NS)
    down = lax.rem(sl + 1, NS)

    def halo(side, to):
        return pltpu.make_async_remote_copy(
            src_ref=hs.at[side], dst_ref=hr.at[1 - side],
            send_sem=hs_sem.at[side], recv_sem=hr_sem.at[1 - side],
            device_id={"slab": to}, device_id_type=MESH,
        )

    halo(0, up).start()
    halo(1, down).start()

    def forward(k, d):
        q = mem_peer(d)
        return pltpu.make_async_remote_copy(
            src_ref=send.at[q, pl.ds(pl.multiple_of(k * ML, ML), ML)],
            dst_ref=recv.at[k, pl.ds(pl.multiple_of(me * ML, ML), ML)],
            send_sem=fs_sem.at[k, d], recv_sem=fr_sem.at[k, me],
            device_id={"mem": q}, device_id_type=MESH,
        )

    def forward_from(k, d):
        q = mem_peer(d)
        return pltpu.make_async_remote_copy(
            src_ref=send.at[q, pl.ds(pl.multiple_of(k * ML, ML), ML)],
            dst_ref=recv.at[k, pl.ds(pl.multiple_of(q * ML, ML), ML)],
            send_sem=fs_sem.at[k, d], recv_sem=fr_sem.at[k, q],
            device_id={"mem": q}, device_id_type=MESH,
        )

    def at_edge(q):
        return jnp.logical_or(q == 0, q == NM - 1)

    @pl.loop(0, K)
    def _(k):
        for d in ORDER:

            @pl.when(jnp.logical_not(at_edge(mem_peer(d))))
            def _():
                forward(k, d).start()

    wt, val = wt_ref[...], val_ref[...]
    mine = lax.broadcasted_iota(jnp.int32, (NS, OBS), 0) == slab_ref[...]
    rows = [jnp.where(mine, piece, 0.0) for piece in parts(wt) + parts(wt * val)]
    left = jnp.concatenate(rows, axis=0).astype(BF16)
    cell = cell_ref[...]
    column = lax.broadcasted_iota(jnp.int32, (W, OBS), 0)
    for p in range(K):
        hot = jnp.where(column + p * W == cell, 1.0, 0.0).astype(BF16)
        sums = nt(left, hot)
        tab[:, p, :] = sums[0:NS] + sums[NS : 2 * NS] + sums[2 * NS : 3 * NS]
        tab[:, K + p, :] = sums[3 * NS : 4 * NS] + sums[4 * NS : 5 * NS] + sums[5 * NS : 6 * NS]

    def route(d):
        to = lax.rem(sl + d, NS)
        return pltpu.make_async_remote_copy(
            src_ref=tab.at[to], dst_ref=orx.at[sl], send_sem=os_sem.at[d], recv_sem=or_sem.at[sl],
            device_id={"slab": to}, device_id_type=MESH,
        )

    def route_from(d):
        to = lax.rem(sl + d, NS)
        return pltpu.make_async_remote_copy(
            src_ref=tab.at[to], dst_ref=orx.at[to], send_sem=os_sem.at[d], recv_sem=or_sem.at[to],
            device_id={"slab": to}, device_id_type=MESH,
        )

    @pl.loop(1, NS)
    def _(d):
        route(d).start()

    orx[sl] = tab[sl]

    pltpu.make_async_remote_copy(
        src_ref=hs.at[0], dst_ref=hr.at[0], send_sem=hs_sem.at[0], recv_sem=hr_sem.at[0],
        device_id={"slab": up}, device_id_type=MESH,
    ).wait_recv()
    pltpu.make_async_remote_copy(
        src_ref=hs.at[1], dst_ref=hr.at[1], send_sem=hs_sem.at[1], recv_sem=hr_sem.at[1],
        device_id={"slab": down}, device_id_type=MESH,
    ).wait_recv()

    def edge(top, a, b, bottom):
        return jnp.concatenate([top, a, b, bottom], axis=0)

    edge_d = edge(hr[0, 16], dif[0:16], dif[112:128], hr[1, 16])
    edge_x = edge(hr[0, 17], vx[0:16], vx[112:128], hr[1, 17])
    edge_y = edge(hr[0, 18], vy[0:16], vy[112:128], hr[1, 18])
    for i, c in enumerate(combine(edge_d, edge_x, edge_y)):
        cfe[i] = c

    @pl.loop(0, ML)
    def _(m):
        x = edge(hr[0, m], ens[m, 0:16, :], ens[m, 112:128, :], hr[1, m])
        x = advance(x, cfe)
        send[0, pl.ds(m, K, stride=ML), :] = x[8:16]
        send[NM - 1, pl.ds(m, K, stride=ML), :] = x[32:40]

    @pl.loop(0, K)
    def _(k):
        for d in ORDER:

            @pl.when(at_edge(mem_peer(d)))
            def _():
                forward(k, d).start()

    @pl.loop(0, K)
    def _(k):
        recv[k, pl.ds(pl.multiple_of(me * ML, ML), ML), :] = send[
            me, pl.ds(pl.multiple_of(k * ML, ML), ML), :
        ]

    @pl.loop(1, NS)
    def _(d):
        route_from(d).wait_recv()

    totals = orx[0]
    for s in range(1, NS):
        totals = totals + orx[s]
    wtot[...] = totals[0:K]
    utot[...] = totals[K : 2 * K]

    def back(k, d):
        q = mem_peer(d)
        return pltpu.make_async_remote_copy(
            src_ref=ana.at[k, pl.ds(pl.multiple_of(q * ML, ML), ML)],
            dst_ref=ret.at[me, pl.ds(pl.multiple_of(k * ML, ML), ML)],
            send_sem=rs_sem.at[k, d], recv_sem=rr_sem.at[k, me],
            device_id={"mem": q}, device_id_type=MESH,
        )

    def back_from(k, d):
        q = mem_peer(d)
        return pltpu.make_async_remote_copy(
            src_ref=ana.at[k, pl.ds(pl.multiple_of(q * ML, ML), ML)],
            dst_ref=ret.at[q, pl.ds(pl.multiple_of(k * ML, ML), ML)],
            send_sem=rs_sem.at[k, d], recv_sem=rr_sem.at[k, q],
            device_id={"mem": q}, device_id_type=MESH,
        )

    eye = jnp.where(
        lax.broadcasted_iota(jnp.int32, (M, M), 0) == lax.broadcasted_iota(jnp.int32, (M, M), 1),
        1.0, 0.0,
    )

    @pl.loop(0, K)
    def _(k):
        @pl.loop(1, NM)
        def _(d):
            forward_from(k, d).wait_recv()

        x = recv[k]
        mean = jnp.sum(x, axis=0, keepdims=True) * (1.0 / M)
        spread = (x - mean).astype(BF16)
        weight = wtot[pl.ds(k, 1), :]
        weighted = (spread.astype(F32) * weight).astype(BF16)
        system = (M - 1.0) * eye + nt(weighted, spread)
        squares = jnp.sum(jnp.sum(system * system, axis=0, keepdims=True), axis=1, keepdims=True)
        scale = 8.0 * jnp.sqrt(squares * (1.0 / M))
        pull = row_times(utot[pl.ds(k, 1), :] - weight * mean, spread)
        iterate = (system * (1.0 / scale)).astype(BF16)
        root = (1.5 * eye - 0.5 * iterate.astype(F32)).astype(BF16)
        iterate = nn(iterate, root).astype(BF16)
        for sweep in range(1, NS_STEPS):
            factor = (1.5 * eye - 0.5 * nn(root, iterate)).astype(BF16)
            if sweep < NS_STEPS - 1:
                iterate = nn(iterate, factor).astype(BF16)
            root = nn(factor, root).astype(BF16)
        gain = row_times(row_times(pull, root), root) * (1.0 / scale)
        transform = (jnp.sqrt((M - 1.0) / scale) * root.astype(F32) + gain).astype(BF16)
        ana[k] = mean + nn(transform, spread)
        for d in ORDER:
            back(k, d).start()
        ret[me, pl.ds(pl.multiple_of(k * ML, ML), ML), :] = ana[
            k, pl.ds(pl.multiple_of(me * ML, ML), ML), :
        ]

    @pl.loop(0, K)
    def _(k):
        @pl.loop(1, NM)
        def _(d):
            back_from(k, d).wait_recv()

    @pl.loop(0, ML)
    def _(m):
        for q in range(NM):
            out_ref[m, q * 8 : q * 8 + 8, :] = ret[q, pl.ds(m, K, stride=ML), :]

    halo(0, up).wait_send()
    halo(1, down).wait_send()

    @pl.loop(1, NS)
    def _(d):
        route(d).wait_send()

    @pl.loop(0, K)
    def _(k):
        @pl.loop(1, NM)
        def _(d):
            forward(k, d).wait_send()
            back(k, d).wait_send()


def shards(ensemble, diffusivity, velocity, obs_value, obs_weight, obs_slab, obs_cell):
    vmem = pl.BlockSpec(memory_space=pltpu.VMEM)
    dma = pltpu.SemaphoreType.DMA
    return pl.pallas_call(
        kernel,
        out_shape=jax.ShapeDtypeStruct((ML, NM * K, W), F32),
        in_specs=[pl.BlockSpec(memory_space=pl.ANY)] + [vmem] * 6,
        out_specs=vmem,
        scratch_shapes=[
            pltpu.VMEM((ML, NM * K, W), F32),
            pltpu.VMEM((5, NM * K, W), F32),
            pltpu.VMEM((5, 48, W), F32),
            pltpu.VMEM((2, ML + 3, 8, W), F32),
            pltpu.VMEM((2, ML + 3, 8, W), F32),
            pltpu.VMEM((NM, K * ML, W), F32),
            pltpu.VMEM((K, M, W), F32),
            pltpu.VMEM((K, M, W), F32),
            pltpu.VMEM((NM, K * ML, W), F32),
            pltpu.VMEM((NS, 2 * K, W), F32),
            pltpu.VMEM((NS, 2 * K, W), F32),
            pltpu.VMEM((K, W), F32),
            pltpu.VMEM((K, W), F32),
            dma,
            dma((2,)),
            dma((2,)),
            dma((K, NM)),
            dma((K, NM)),
            dma((K, NM)),
            dma((K, NM)),
            dma((NS,)),
            dma((NS,)),
        ],
        compiler_params=pltpu.CompilerParams(
            collective_id=0, has_side_effects=True, vmem_limit_bytes=40 * 2**20
        ),
    )(
        ensemble,
        diffusivity,
        velocity,
        obs_value.reshape(1, OBS),
        obs_weight.reshape(1, OBS),
        obs_slab.reshape(1, OBS),
        obs_cell.reshape(1, OBS),
    )


def solution(mesh):
    return jax.shard_map(
        shards,
        mesh=mesh,
        in_specs=(
            P("mem", "slab", None),
            P("slab", None),
            P(None, "slab", None),
            P(("mem", "slab")),
            P(("mem", "slab")),
            P(("mem", "slab"), None),
            P(("mem", "slab")),
        ),
        out_specs=P("mem", "slab", None),
        check_vma=False,
    )
```

time: 228 us -> 123 us (0.54)
  the two profiles are of different devices: /device:TPU:2 before, /device:TPU:1 now
where the time goes in v1:
time: 123 us; the launch traced here: 122 us
  Pallas kernels  115 us (93%)
  local copies, waits for them, and re-layouts  6.03 us (5%)
    pallas_call x1, Pallas kernels, shards(): pl.pallas_call(kernel, out_shape=jax.ShapeDtypeStruct((ML, NM * K, W), F3...  115 us
    unnamed x13, local copies, waits for them, and re-layouts  5.31 us

profile of v1, /device:TPU:1, one launch (start us, length us, event | category | flops | bytes accessed | tf_op | source)
XLA Modules:
  0.0 121.5 jit_solution(5764815889770408488)
XLA Ops:
  0.0 0.0 copy-start.4
  0.0 0.7 reshape.12.val_ref
  0.7 0.0 copy-done.4
  0.7 0.0 copy-start.5
  0.7 0.7 copy-done.5
  1.4 0.0 copy-start.3
  1.4 0.7 copy-done.3
  2.1 0.0 copy-start
  2.1 1.2 %copy-done = f32[16,128,128]{2,1,0:T(8,128)S(1)} copy-done((f32[16,128,128]{2,1,0:T(8,128)S(1)}, f32[16,128,128]{2,1,0:T(8,128)}, u32[]{:S(2)}) %copy-start) | copy-done | bytes 1048600
  3.3 0.0 copy-start.1
  3.3 0.9 copy-done.1
  4.2 0.0 copy-start.2
  4.2 0.8 copy-done.2
  5.1 115.5 %shard_map.73 = f32[16,128,128]{2,1,0:T(8,128)S(1)} custom-call(f32[16,128,128]{2,1,0:T(8,128)S(1)} %copy-done, f32[128,128]{1,0:T(8,128)S(1)} %copy-done.2, f32[2,128,128]{2,1,0:T(8,128)S(1)} %copy-done.1, f32[1,1280]{1,0:T(1,128)S(1)} %reshape.12.val_ref, f32[1,1280]{1,0:T(1,128)S(1)} %reshape.13.wt_ref, s32[1,1280]{1,0:T(1,128)S(1)} %bitcast.1, ...), custom_call_target="tpu_custom_call" | custom-call | tf_op jit(solution)/shard_map/pallas_call | solution.py:322
  120.5 1.0 copy.9
  (2 shorter events, 0.0 us)
Async XLA Ops:
  0.0 0.7 copy-start.4
  0.7 0.7 copy-start.5
  1.4 0.7 copy-start.3
  2.1 1.2 %copy-start = (f32[16,128,128]{2,1,0:T(8,128)S(1)}, f32[16,128,128]{2,1,0:T(8,128)}, u32[]{:S(2)}) copy-start(f32[16,128,128]{2,1,0:T(8,128)} %ens_ref.1) | copy-start | bytes 3145732
  3.3 0.9 copy-start.1
  4.2 0.8 copy-start.2

commit v2 on v1

--- a/solution.py
+++ b/solution.py
@@ -14,6 +14,10 @@
 ML = 16
 W = 128
 OBS = 1280
+ROWS = 128
+HALO = 4
+EARLY = 2
+PIECES, STRIDE, QS = 3, 40, 5
 MESH = pl.DeviceIdType.MESH
 F32 = jnp.float32
 BF16 = jnp.bfloat16
@@ -47,17 +51,16 @@
     return jnp.sum(nt(stack.astype(BF16), mat_t), axis=0, keepdims=True)
 
 
-def advance(x, coeffs):
-    rows = x.shape[0]
-    for _ in range(STEPS):
-        x = (
-            coeffs[0] * x
-            + coeffs[1] * pltpu.roll(x, W - 1, 1)
-            + coeffs[2] * pltpu.roll(x, 1, 1)
-            + coeffs[3] * pltpu.roll(x, 1, 0)
-            + coeffs[4] * pltpu.roll(x, rows - 1, 0)
-        )
-    return x
+def advance(src, dst, cx, at, rows, shift=0):
+    for r in range(rows):
+        c = [cx[i, at + r] for i in range(5)]
+        for h in range(2):
+            x = src[at + r, h]
+            dst[at + r + shift, h] = (
+                (c[0] * x + c[3] * src[at + r - 1, h])
+                + (c[4] * src[at + r + 1, h] + c[1] * pltpu.roll(x, W - 1, 1))
+                + c[2] * pltpu.roll(x, 1, 1)
+            )
 
 
 def combine(d, vx, vy):
@@ -66,9 +69,9 @@
 
 
 def kernel(
-    ens_ref, dif_ref, vel_ref, val_ref, wt_ref, slab_ref, cell_ref, out_ref,
-    ens, cf, cfe, hs, hr, send, recv, ana, ret, tab, orx, wtot, utot,
-    ens_sem, hs_sem, hr_sem, fs_sem, fr_sem, rs_sem, rr_sem, os_sem, or_sem,
+    ens_hbm, dif_hbm, vel_hbm, val_hbm, wt_hbm, slab_hbm, cell_hbm, out_ref,
+    ens, dif_ref, vel_ref, val_ref, wt_ref, slab_ref, cell_ref, b0, b1, b2, b3, cx, cs, cr, send, recv, ana, ret, tab, orx, wtot, utot,
+    in_sem, hs_sem, hr_sem, cs_sem, cr_sem, fs_sem, fr_sem, rs_sem, rr_sem, os_sem, or_sem,
 ):
     me = lax.axis_index("mem")
     sl = lax.axis_index("slab")
@@ -76,8 +79,13 @@
     def mem_peer(d):
         return lax.rem(me + d, NM)
 
-    load = pltpu.make_async_copy(ens_ref, ens, ens_sem)
-    load.start()
+    pairs = (
+        (dif_hbm, dif_ref), (vel_hbm, vel_ref), (ens_hbm, ens),
+        (wt_hbm, wt_ref), (val_hbm, val_ref), (slab_hbm, slab_ref), (cell_hbm, cell_ref),
+    )
+    loads = [pltpu.make_async_copy(a, b, in_sem.at[i]) for i, (a, b) in enumerate(pairs)]
+    for load in loads:
+        load.start()
     bar = pltpu.get_barrier_semaphore()
 
     @pl.loop(1, NM)
@@ -90,46 +98,54 @@
             bar, inc=1, device_id={"slab": lax.rem(sl + d, NS)}, device_id_type=MESH
         )
 
-    dif, vx, vy = dif_ref[...], vel_ref[0], vel_ref[1]
-    for i, c in enumerate(combine(dif, vx, vy)):
-        cf[i] = c
-    hs[0, 16], hs[1, 16] = dif[0:8], dif[120:128]
-    hs[0, 17], hs[1, 17] = vx[0:8], vx[120:128]
-    hs[0, 18], hs[1, 18] = vy[0:8], vy[120:128]
-    load.wait()
-
-    @pl.loop(0, ML)
-    def _(m):
-        x = ens[m]
-        hs[0, m] = x[0:8]
-        hs[1, m] = x[120:128]
-
-    @pl.loop(0, ML)
-    def _(m):
-        x = advance(ens[m], cf)
-        for q in range(1, NM - 1):
-            send[q, pl.ds(m, K, stride=ML), :] = x[q * 8 : q * 8 + 8]
-
-    pl.semaphore_wait(bar, NM - 1 + NS - 1)
+    loads[0].wait()
+    loads[1].wait()
+    for i, ref in enumerate((dif_ref, vel_ref.at[0], vel_ref.at[1])):
+        cs[0, i] = ref[0:8]
+        cs[1, i] = ref[120:128]
+
+    def expand(at, rows, d, vx, vy):
+        for i, c in enumerate(combine(d, vx, vy)):
+            cx[i, pl.ds(at, rows)] = jnp.broadcast_to(c[:, None, :], (rows, 8, W))
+
+    @pl.loop(0, NM)
+    def _(b):
+        own = pl.ds(pl.multiple_of(b * 8, 8), 8)
+        expand(HALO + b * 8, 8, dif_ref[own], vel_ref[0, own], vel_ref[1, own])
+
+    loads[2].wait()
+
+    @pl.loop(0, NM)
+    def _(b):
+        for h in range(2):
+            tiles = [
+                ens[pl.ds(pl.multiple_of((h * 8 + m) * ROWS + b * 8, 8), 8), :] for m in range(8)
+            ]
+            b0[pl.ds(HALO + b * 8, 8), h] = jnp.swapaxes(jnp.stack(tiles, axis=0), 0, 1)
 
     up = lax.rem(sl + NS - 1, NS)
     down = lax.rem(sl + 1, NS)
 
     def halo(side, to):
-        return pltpu.make_async_remote_copy(
-            src_ref=hs.at[side], dst_ref=hr.at[1 - side],
-            send_sem=hs_sem.at[side], recv_sem=hr_sem.at[1 - side],
+        start, land = ((HALO, HALO + ROWS), (ROWS, 0))[side]
+        fields = pltpu.make_async_remote_copy(
+            src_ref=b0.at[pl.ds(start, HALO)], dst_ref=b0.at[pl.ds(land, HALO)],
+            send_sem=hs_sem.at[side], recv_sem=hr_sem.at[side],
             device_id={"slab": to}, device_id_type=MESH,
         )
-
-    halo(0, up).start()
-    halo(1, down).start()
+        coeffs = pltpu.make_async_remote_copy(
+            src_ref=cs.at[side], dst_ref=cr.at[side],
+            send_sem=cs_sem.at[side], recv_sem=cr_sem.at[side],
+            device_id={"slab": to}, device_id_type=MESH,
+        )
+        return fields, coeffs
+
+    halos = halo(0, up) + halo(1, down)
 
     def forward(k, d):
         q = mem_peer(d)
         return pltpu.make_async_remote_copy(
-            src_ref=send.at[q, pl.ds(pl.multiple_of(k * ML, ML), ML)],
-            dst_ref=recv.at[k, pl.ds(pl.multiple_of(me * ML, ML), ML)],
+            src_ref=send.at[q * K + k], dst_ref=recv.at[k, pl.ds(2 * me, 2)],
             send_sem=fs_sem.at[k, d], recv_sem=fr_sem.at[k, me],
             device_id={"mem": q}, device_id_type=MESH,
         )
@@ -137,28 +153,48 @@
     def forward_from(k, d):
         q = mem_peer(d)
         return pltpu.make_async_remote_copy(
-            src_ref=send.at[q, pl.ds(pl.multiple_of(k * ML, ML), ML)],
-            dst_ref=recv.at[k, pl.ds(pl.multiple_of(q * ML, ML), ML)],
+            src_ref=send.at[q * K + k], dst_ref=recv.at[k, pl.ds(2 * q, 2)],
             send_sem=fs_sem.at[k, d], recv_sem=fr_sem.at[k, q],
             device_id={"mem": q}, device_id_type=MESH,
         )
 
-    def at_edge(q):
-        return jnp.logical_or(q == 0, q == NM - 1)
-
-    @pl.loop(0, K)
-    def _(k):
-        for d in ORDER:
-
-            @pl.when(jnp.logical_not(at_edge(mem_peer(d))))
-            def _():
-                forward(k, d).start()
-
-    wt, val = wt_ref[...], val_ref[...]
+    def at_edge(k, q):
+        return q == 0 if k < HALO else q == NM - 1
+
+    states = (b0, b1, b2, b3, send)
+
+    @pl.loop(0, PIECES)
+    def _(b):
+        for step in range(STEPS):
+            first = HALO + step + 1
+            rows = ROWS - 2 * step - 2 - (PIECES - 1) * STRIDE
+            shift = -HALO if step == STEPS - 1 else 0
+            advance(states[step], states[step + 1], cx, first + b * STRIDE, rows, shift)
+
+        @pl.when(b == 0)
+        def _():
+            pl.semaphore_wait(bar, NM - 1 + NS - 1)
+            for copy in halos:
+                copy.start()
+
+        for k in range(EARLY):
+            for i in range(QS):
+                q = b * QS + i
+
+                @pl.when(jnp.logical_and(q != me, jnp.logical_not(at_edge(k, q))))
+                def _():
+                    forward(k, lax.rem(q - me + NM, NM)).start()
+
+    for load in loads[3:]:
+        load.wait()
+
+    def row(ref):
+        return jnp.concatenate([ref[i : i + 1, :] for i in range(OBS // W)], axis=1)
+
+    wt, val, cell = row(wt_ref), row(val_ref), row(cell_ref)
     mine = lax.broadcasted_iota(jnp.int32, (NS, OBS), 0) == slab_ref[...]
     rows = [jnp.where(mine, piece, 0.0) for piece in parts(wt) + parts(wt * val)]
     left = jnp.concatenate(rows, axis=0).astype(BF16)
-    cell = cell_ref[...]
     column = lax.broadcasted_iota(jnp.int32, (W, OBS), 0)
     for p in range(K):
         hot = jnp.where(column + p * W == cell, 1.0, 0.0).astype(BF16)
@@ -186,44 +222,32 @@
 
     orx[sl] = tab[sl]
 
-    pltpu.make_async_remote_copy(
-        src_ref=hs.at[0], dst_ref=hr.at[0], send_sem=hs_sem.at[0], recv_sem=hr_sem.at[0],
-        device_id={"slab": up}, device_id_type=MESH,
-    ).wait_recv()
-    pltpu.make_async_remote_copy(
-        src_ref=hs.at[1], dst_ref=hr.at[1], send_sem=hs_sem.at[1], recv_sem=hr_sem.at[1],
-        device_id={"slab": down}, device_id_type=MESH,
-    ).wait_recv()
-
-    def edge(top, a, b, bottom):
-        return jnp.concatenate([top, a, b, bottom], axis=0)
-
-    edge_d = edge(hr[0, 16], dif[0:16], dif[112:128], hr[1, 16])
-    edge_x = edge(hr[0, 17], vx[0:16], vx[112:128], hr[1, 17])
-    edge_y = edge(hr[0, 18], vy[0:16], vy[112:128], hr[1, 18])
-    for i, c in enumerate(combine(edge_d, edge_x, edge_y)):
-        cfe[i] = c
-
-    @pl.loop(0, ML)
-    def _(m):
-        x = edge(hr[0, m], ens[m, 0:16, :], ens[m, 112:128, :], hr[1, m])
-        x = advance(x, cfe)
-        send[0, pl.ds(m, K, stride=ML), :] = x[8:16]
-        send[NM - 1, pl.ds(m, K, stride=ML), :] = x[32:40]
+    for copy in halos:
+        copy.wait_recv()
+    tail = pl.ds(8 - HALO, HALO)
+    expand(0, HALO, cr[1, 0, tail], cr[1, 1, tail], cr[1, 2, tail])
+    expand(HALO + ROWS, HALO, cr[0, 0, 0:HALO], cr[0, 1, 0:HALO], cr[0, 2, 0:HALO])
+    for step in range(STEPS):
+        src, dst = states[step], states[step + 1]
+        shift = -HALO if step == STEPS - 1 else 0
+        advance(src, dst, cx, step + 1, HALO, shift)
+        advance(src, dst, cx, HALO + ROWS - step - 1, HALO, shift)
+
+    for k in range(EARLY):
+        for d in ORDER:
+
+            @pl.when(jnp.logical_or(at_edge(k, mem_peer(d)), mem_peer(d) >= PIECES * QS))
+            def _():
+                forward(k, d).start()
+
+    @pl.loop(EARLY, K)
+    def _(k):
+        for d in ORDER:
+            forward(k, d).start()
 
     @pl.loop(0, K)
     def _(k):
-        for d in ORDER:
-
-            @pl.when(at_edge(mem_peer(d)))
-            def _():
-                forward(k, d).start()
-
-    @pl.loop(0, K)
-    def _(k):
-        recv[k, pl.ds(pl.multiple_of(me * ML, ML), ML), :] = send[
-            me, pl.ds(pl.multiple_of(k * ML, ML), ML), :
-        ]
+        recv[k, pl.ds(2 * me, 2)] = send[me * K + k]
 
     @pl.loop(1, NS)
     def _(d):
@@ -264,7 +288,7 @@
         def _(d):
             forward_from(k, d).wait_recv()
 
-        x = recv[k]
+        x = recv[k].reshape(M, W)
         mean = jnp.sum(x, axis=0, keepdims=True) * (1.0 / M)
         spread = (x - mean).astype(BF16)
         weight = wtot[pl.ds(k, 1), :]
@@ -301,8 +325,8 @@
         for q in range(NM):
             out_ref[m, q * 8 : q * 8 + 8, :] = ret[q, pl.ds(m, K, stride=ML), :]
 
-    halo(0, up).wait_send()
-    halo(1, down).wait_send()
+    for copy in halos:
+        copy.wait_send()
 
     @pl.loop(1, NS)
     def _(d):
@@ -322,23 +346,34 @@
     return pl.pallas_call(
         kernel,
         out_shape=jax.ShapeDtypeStruct((ML, NM * K, W), F32),
-        in_specs=[pl.BlockSpec(memory_space=pl.ANY)] + [vmem] * 6,
+        in_specs=[pl.BlockSpec(memory_space=pltpu.HBM)] * 7,
         out_specs=vmem,
         scratch_shapes=[
-            pltpu.VMEM((ML, NM * K, W), F32),
-            pltpu.VMEM((5, NM * K, W), F32),
-            pltpu.VMEM((5, 48, W), F32),
-            pltpu.VMEM((2, ML + 3, 8, W), F32),
-            pltpu.VMEM((2, ML + 3, 8, W), F32),
-            pltpu.VMEM((NM, K * ML, W), F32),
-            pltpu.VMEM((K, M, W), F32),
+            pltpu.VMEM((ML * ROWS, W), F32),
+            pltpu.VMEM((NM * K, W), F32),
+            pltpu.VMEM((2, NM * K, W), F32),
+            pltpu.VMEM((OBS // W, W), F32),
+            pltpu.VMEM((OBS // W, W), F32),
+            pltpu.VMEM((1, OBS), jnp.int32),
+            pltpu.VMEM((OBS // W, W), jnp.int32),
+            pltpu.VMEM((ROWS + 2 * HALO, 2, 8, W), F32),
+            pltpu.VMEM((ROWS + 2 * HALO, 2, 8, W), F32),
+            pltpu.VMEM((ROWS + 2 * HALO, 2, 8, W), F32),
+            pltpu.VMEM((ROWS + 2 * HALO, 2, 8, W), F32),
+            pltpu.VMEM((5, ROWS + 2 * HALO, 8, W), F32),
+            pltpu.VMEM((2, 3, 8, W), F32),
+            pltpu.VMEM((2, 3, 8, W), F32),
+            pltpu.VMEM((ROWS, 2, 8, W), F32),
+            pltpu.VMEM((K, 2 * NM, 8, W), F32),
             pltpu.VMEM((K, M, W), F32),
             pltpu.VMEM((NM, K * ML, W), F32),
             pltpu.VMEM((NS, 2 * K, W), F32),
             pltpu.VMEM((NS, 2 * K, W), F32),
             pltpu.VMEM((K, W), F32),
             pltpu.VMEM((K, W), F32),
-            dma,
+            dma((7,)),
+            dma((2,)),
+            dma((2,)),
             dma((2,)),
             dma((2,)),
             dma((K, NM)),
@@ -349,16 +384,16 @@
             dma((NS,)),
         ],
         compiler_params=pltpu.CompilerParams(
-            collective_id=0, has_side_effects=True, vmem_limit_bytes=40 * 2**20
+            collective_id=0, has_side_effects=True, vmem_limit_bytes=62 * 2**20
         ),
     )(
-        ensemble,
+        ensemble.reshape(ML * ROWS, W),
         diffusivity,
         velocity,
-        obs_value.reshape(1, OBS),
-        obs_weight.reshape(1, OBS),
+        obs_value.reshape(OBS // W, W),
+        obs_weight.reshape(OBS // W, W),
         obs_slab.reshape(1, OBS),
-        obs_cell.reshape(1, OBS),
+        obs_cell.reshape(OBS // W, W),
     )
 
 

time: 123 us -> 121 us (0.984)
  local copies, waits for them, and re-layouts: 6.03 us -> 2.3 us
  Pallas kernels: 115 us -> 118 us
    unnamed x13 -> x1, local copies, waits for them, and re-layouts: 5.31 us -> 2.3 us
    pallas_call x1, Pallas kernels: 115 us -> 118 us  [shards(): pl.pallas_call(kernel, out_shape=jax.ShapeDtypeStruct((ML, NM * K, W), F3...]
where the time goes in v2:
time: 121 us
  Pallas kernels  118 us (98%)
  local copies, waits for them, and re-layouts  2.3 us (2%)
    pallas_call x1, Pallas kernels, shards(): pl.pallas_call(kernel, out_shape=jax.ShapeDtypeStruct((ML, NM * K, W), F3...  118 us

profile of v2, /device:TPU:1, one launch (start us, length us, event | category | flops | bytes accessed | tf_op | source)
XLA Modules:
  0.0 120.6 jit_solution(4841448712448723151)
XLA Ops:
  0.0 118.3 %shard_map.73 = f32[16,128,128]{2,1,0:T(8,128)} custom-call(f32[2048,128]{1,0:T(8,128)} %bitcast.5, f32[128,128]{1,0:T(8,128)} %dif_hbm.1, f32[2,128,128]{2,1,0:T(8,128)} %vel_hbm.1, f32[10,128]{1,0:T(8,128)} %bitcast.6, f32[10,128]{1,0:T(8,128)} %bitcast.7, s32[1,1280]{1,0:T(1,128)} %bitcast.9, s32[10,128]{1,0:T(8,128)} %bitcast.8), custom_call_target="tpu_custom_call" | custom-call | tf_op jit(solution)/shard_map/pallas_call | solution.py:346
  118.3 2.3 %copy.9 = f32[16,128,128]{2,1,0:T(8,128)} copy(f32[16,128,128]{2,1,0:T(8,128)} %shard_map.73) | data formatting | bytes 2097152

commit v3 on v2

--- a/solution.py
+++ b/solution.py
@@ -16,7 +16,9 @@
 OBS = 1280
 ROWS = 128
 HALO = 4
-EARLY = 2
+GF, GB = 4, 4
+FG, BG, PAIRS = K // GF, K // GB, K // 2
+EARLY = 1
 PIECES, STRIDE, QS = 3, 40, 5
 MESH = pl.DeviceIdType.MESH
 F32 = jnp.float32
@@ -145,7 +147,7 @@
     def forward(k, d):
         q = mem_peer(d)
         return pltpu.make_async_remote_copy(
-            src_ref=send.at[q * K + k], dst_ref=recv.at[k, pl.ds(2 * me, 2)],
+            src_ref=send.at[pl.ds(q * K + GF * k, GF)], dst_ref=recv.at[k, me],
             send_sem=fs_sem.at[k, d], recv_sem=fr_sem.at[k, me],
             device_id={"mem": q}, device_id_type=MESH,
         )
@@ -153,13 +155,15 @@
     def forward_from(k, d):
         q = mem_peer(d)
         return pltpu.make_async_remote_copy(
-            src_ref=send.at[q * K + k], dst_ref=recv.at[k, pl.ds(2 * q, 2)],
+            src_ref=send.at[pl.ds(q * K + GF * k, GF)], dst_ref=recv.at[k, q],
             send_sem=fs_sem.at[k, d], recv_sem=fr_sem.at[k, q],
             device_id={"mem": q}, device_id_type=MESH,
         )
 
     def at_edge(k, q):
-        return q == 0 if k < HALO else q == NM - 1
+        low = q == 0 if GF * k < HALO else False
+        high = q == NM - 1 if GF * (k + 1) > HALO else False
+        return jnp.logical_or(low, high)
 
     states = (b0, b1, b2, b3, send)
 
@@ -240,14 +244,14 @@
             def _():
                 forward(k, d).start()
 
-    @pl.loop(EARLY, K)
+    @pl.loop(EARLY, FG)
     def _(k):
         for d in ORDER:
             forward(k, d).start()
 
-    @pl.loop(0, K)
+    @pl.loop(0, FG)
     def _(k):
-        recv[k, pl.ds(2 * me, 2)] = send[me * K + k]
+        recv[k, me] = send[pl.ds(me * K + GF * k, GF)]
 
     @pl.loop(1, NS)
     def _(d):
@@ -262,8 +266,7 @@
     def back(k, d):
         q = mem_peer(d)
         return pltpu.make_async_remote_copy(
-            src_ref=ana.at[k, pl.ds(pl.multiple_of(q * ML, ML), ML)],
-            dst_ref=ret.at[me, pl.ds(pl.multiple_of(k * ML, ML), ML)],
+            src_ref=ana.at[k, q], dst_ref=ret.at[me, pl.ds(pl.multiple_of(k * GB * ML, GB * ML), GB * ML)],
             send_sem=rs_sem.at[k, d], recv_sem=rr_sem.at[k, me],
             device_id={"mem": q}, device_id_type=MESH,
         )
@@ -271,8 +274,7 @@
     def back_from(k, d):
         q = mem_peer(d)
         return pltpu.make_async_remote_copy(
-            src_ref=ana.at[k, pl.ds(pl.multiple_of(q * ML, ML), ML)],
-            dst_ref=ret.at[q, pl.ds(pl.multiple_of(k * ML, ML), ML)],
+            src_ref=ana.at[k, q], dst_ref=ret.at[q, pl.ds(pl.multiple_of(k * GB * ML, GB * ML), GB * ML)],
             send_sem=rs_sem.at[k, d], recv_sem=rr_sem.at[k, q],
             device_id={"mem": q}, device_id_type=MESH,
         )
@@ -282,39 +284,58 @@
         1.0, 0.0,
     )
 
-    @pl.loop(0, K)
+    def one_and_half(product):
+        return (1.5 * eye - 0.5 * product).astype(BF16)
+
+    @pl.loop(0, PAIRS)
     def _(k):
-        @pl.loop(1, NM)
-        def _(d):
-            forward_from(k, d).wait_recv()
-
-        x = recv[k].reshape(M, W)
-        mean = jnp.sum(x, axis=0, keepdims=True) * (1.0 / M)
-        spread = (x - mean).astype(BF16)
-        weight = wtot[pl.ds(k, 1), :]
-        weighted = (spread.astype(F32) * weight).astype(BF16)
-        system = (M - 1.0) * eye + nt(weighted, spread)
-        squares = jnp.sum(jnp.sum(system * system, axis=0, keepdims=True), axis=1, keepdims=True)
-        scale = 8.0 * jnp.sqrt(squares * (1.0 / M))
-        pull = row_times(utot[pl.ds(k, 1), :] - weight * mean, spread)
-        iterate = (system * (1.0 / scale)).astype(BF16)
-        root = (1.5 * eye - 0.5 * iterate.astype(F32)).astype(BF16)
-        iterate = nn(iterate, root).astype(BF16)
+        group = k // (GF // 2)
+        place = 2 * (k % (GF // 2))
+
+        @pl.when(place == 0)
+        def _():
+            @pl.loop(1, NM)
+            def _(d):
+                forward_from(group, d).wait_recv()
+
+        two = range(2)
+        x = [recv[group, :, place + j].reshape(M, W) for j in two]
+        mean = [jnp.sum(x[j], axis=0, keepdims=True) * (1.0 / M) for j in two]
+        spread = [(x[j] - mean[j]).astype(BF16) for j in two]
+        weight = [wtot[pl.ds(2 * k + j, 1), :] for j in two]
+        weighted = [(spread[j].astype(F32) * weight[j]).astype(BF16) for j in two]
+        system = [(M - 1.0) * eye + nt(weighted[j], spread[j]) for j in two]
+        squares = [
+            jnp.sum(jnp.sum(a * a, axis=0, keepdims=True), axis=1, keepdims=True) for a in system
+        ]
+        scale = [8.0 * jnp.sqrt(a * (1.0 / M)) for a in squares]
+        pull = [
+            row_times(utot[pl.ds(2 * k + j, 1), :] - weight[j] * mean[j], spread[j]) for j in two
+        ]
+        iterate = [(system[j] * (1.0 / scale[j])).astype(BF16) for j in two]
+        root = [one_and_half(iterate[j].astype(F32)) for j in two]
+        iterate = [nn(iterate[j], root[j]).astype(BF16) for j in two]
         for sweep in range(1, NS_STEPS):
-            factor = (1.5 * eye - 0.5 * nn(root, iterate)).astype(BF16)
+            factor = [one_and_half(nn(root[j], iterate[j])) for j in two]
             if sweep < NS_STEPS - 1:
-                iterate = nn(iterate, factor).astype(BF16)
-            root = nn(factor, root).astype(BF16)
-        gain = row_times(row_times(pull, root), root) * (1.0 / scale)
-        transform = (jnp.sqrt((M - 1.0) / scale) * root.astype(F32) + gain).astype(BF16)
-        ana[k] = mean + nn(transform, spread)
-        for d in ORDER:
-            back(k, d).start()
-        ret[me, pl.ds(pl.multiple_of(k * ML, ML), ML), :] = ana[
-            k, pl.ds(pl.multiple_of(me * ML, ML), ML), :
-        ]
-
-    @pl.loop(0, K)
+                iterate = [nn(iterate[j], factor[j]).astype(BF16) for j in two]
+            root = [nn(factor[j], root[j]).astype(BF16) for j in two]
+        first = [row_times(pull[j], root[j]) for j in two]
+        gain = [row_times(first[j], root[j]) * (1.0 / scale[j]) for j in two]
+        for j in two:
+            transform = (jnp.sqrt((M - 1.0) / scale[j]) * root[j].astype(F32) + gain[j]).astype(BF16)
+            result = mean[j] + nn(transform, spread[j])
+            at = (2 * (k % (GB // 2)) + j) * ML
+            ana[k // (GB // 2), :, pl.ds(pl.multiple_of(at, ML), ML)] = result.reshape(NM, ML, W)
+
+        @pl.when(k % (GB // 2) == GB // 2 - 1)
+        def _():
+            out = k // (GB // 2)
+            for d in ORDER:
+                back(out, d).start()
+            ret[me, pl.ds(pl.multiple_of(out * GB * ML, GB * ML), GB * ML), :] = ana[out, me]
+
+    @pl.loop(0, BG)
     def _(k):
         @pl.loop(1, NM)
         def _(d):
@@ -332,11 +353,14 @@
     def _(d):
         route(d).wait_send()
 
-    @pl.loop(0, K)
-    def _(k):
-        @pl.loop(1, NM)
-        def _(d):
+    @pl.loop(1, NM)
+    def _(d):
+        @pl.loop(0, FG)
+        def _(k):
             forward(k, d).wait_send()
+
+        @pl.loop(0, BG)
+        def _(k):
             back(k, d).wait_send()
 
 
@@ -364,8 +388,8 @@
             pltpu.VMEM((2, 3, 8, W), F32),
             pltpu.VMEM((2, 3, 8, W), F32),
             pltpu.VMEM((ROWS, 2, 8, W), F32),
-            pltpu.VMEM((K, 2 * NM, 8, W), F32),
-            pltpu.VMEM((K, M, W), F32),
+            pltpu.VMEM((FG, NM, GF, 2, 8, W), F32),
+            pltpu.VMEM((BG, NM, GB * ML, W), F32),
             pltpu.VMEM((NM, K * ML, W), F32),
             pltpu.VMEM((NS, 2 * K, W), F32),
             pltpu.VMEM((NS, 2 * K, W), F32),
@@ -376,10 +400,10 @@
             dma((2,)),
             dma((2,)),
             dma((2,)),
-            dma((K, NM)),
-            dma((K, NM)),
-            dma((K, NM)),
-            dma((K, NM)),
+            dma((FG, NM)),
+            dma((FG, NM)),
+            dma((BG, NM)),
+            dma((BG, NM)),
             dma((NS,)),
             dma((NS,)),
         ],

time: 121 us -> 115 us (0.950)
  Pallas kernels: 118 us -> 112 us
    pallas_call x1, Pallas kernels: 118 us -> 112 us  [shards(): pl.pallas_call(kernel, out_shape=jax.ShapeDtypeStruct((ML, NM * K, W), F3...]
where the time goes in v3:
time: 115 us; the launch traced here: 114 us
  Pallas kernels  112 us (97%)
  local copies, waits for them, and re-layouts  2.3 us (2%)
    pallas_call x1, Pallas kernels, shards(): pl.pallas_call(kernel, out_shape=jax.ShapeDtypeStruct((ML, NM * K, W), F3...  112 us

profile of v3, /device:TPU:1, one launch (start us, length us, event | category | flops | bytes accessed | tf_op | source)
XLA Modules:
  0.0 114.4 jit_solution(13017217112380622371)
XLA Ops:
  0.0 112.1 %shard_map.73 = f32[16,128,128]{2,1,0:T(8,128)} custom-call(f32[2048,128]{1,0:T(8,128)} %bitcast.5, f32[128,128]{1,0:T(8,128)} %dif_hbm.1, f32[2,128,128]{2,1,0:T(8,128)} %vel_hbm.1, f32[10,128]{1,0:T(8,128)} %bitcast.6, f32[10,128]{1,0:T(8,128)} %bitcast.7, s32[1,1280]{1,0:T(1,128)} %bitcast.9, s32[10,128]{1,0:T(8,128)} %bitcast.8), custom_call_target="tpu_custom_call" | custom-call | tf_op jit(solution)/shard_map/pallas_call | solution.py:370
  112.1 2.3 %copy.9 = f32[16,128,128]{2,1,0:T(8,128)} copy(f32[16,128,128]{2,1,0:T(8,128)} %shard_map.73) | data formatting | bytes 2097152

commit v4 on v3

--- a/solution.py
+++ b/solution.py
@@ -18,6 +18,8 @@
 HALO = 4
 GF, GB = 4, 4
 FG, BG, PAIRS = K // GF, K // GB, K // 2
+BACK = ((0, 0, 64), (1, 0, 32), (1, 32, 32))
+QB = 8
 EARLY = 1
 PIECES, STRIDE, QS = 3, 40, 5
 MESH = pl.DeviceIdType.MESH
@@ -71,9 +73,9 @@
 
 
 def kernel(
-    ens_hbm, dif_hbm, vel_hbm, val_hbm, wt_hbm, slab_hbm, cell_hbm, out_ref,
-    ens, dif_ref, vel_ref, val_ref, wt_ref, slab_ref, cell_ref, b0, b1, b2, b3, cx, cs, cr, send, recv, ana, ret, tab, orx, wtot, utot,
-    in_sem, hs_sem, hr_sem, cs_sem, cr_sem, fs_sem, fr_sem, rs_sem, rr_sem, os_sem, or_sem,
+    ens_hbm, dif_hbm, vel_hbm, val_hbm, wt_hbm, slab_hbm, cell_hbm, ret,
+    ens, dif_ref, vel_ref, val_ref, wt_ref, slab_ref, cell_ref, b0, b1, b2, b3, cx, cs, cr, send, recv, ana, tab, orx, wtot, utot,
+    in_sem, hs_sem, hr_sem, cs_sem, cr_sem, fs_sem, fr_sem, rs_sem, rr_sem, os_sem, or_sem, own_sem,
 ):
     me = lax.axis_index("mem")
     sl = lax.axis_index("slab")
@@ -263,21 +265,25 @@
     wtot[...] = totals[0:K]
     utot[...] = totals[K : 2 * K]
 
-    def back(k, d):
+    def back_by(n, d, source):
+        k, start, rows = BACK[n]
         q = mem_peer(d)
+        land = pl.ds(k * GB * ML + start, rows)
         return pltpu.make_async_remote_copy(
-            src_ref=ana.at[k, q], dst_ref=ret.at[me, pl.ds(pl.multiple_of(k * GB * ML, GB * ML), GB * ML)],
-            send_sem=rs_sem.at[k, d], recv_sem=rr_sem.at[k, me],
+            src_ref=ana.at[k, q, pl.ds(start, rows)], dst_ref=ret.at[source, land],
+            send_sem=rs_sem.at[n, d], recv_sem=rr_sem.at[n, source],
             device_id={"mem": q}, device_id_type=MESH,
         )
 
-    def back_from(k, d):
-        q = mem_peer(d)
-        return pltpu.make_async_remote_copy(
-            src_ref=ana.at[k, q], dst_ref=ret.at[q, pl.ds(pl.multiple_of(k * GB * ML, GB * ML), GB * ML)],
-            send_sem=rs_sem.at[k, d], recv_sem=rr_sem.at[k, q],
-            device_id={"mem": q}, device_id_type=MESH,
-        )
+    def back(n, d):
+        return back_by(n, d, me)
+
+    def back_from(n, d):
+        return back_by(n, d, mem_peer(d))
+
+    def own(k):
+        place = pl.ds(pl.multiple_of(k * GB * ML, GB * ML), GB * ML)
+        return pltpu.make_async_copy(ana.at[k, me], ret.at[me, place], own_sem.at[k])
 
     eye = jnp.where(
         lax.broadcasted_iota(jnp.int32, (M, M), 0) == lax.broadcasted_iota(jnp.int32, (M, M), 1),
@@ -328,23 +334,26 @@
             at = (2 * (k % (GB // 2)) + j) * ML
             ana[k // (GB // 2), :, pl.ds(pl.multiple_of(at, ML), ML)] = result.reshape(NM, ML, W)
 
-        @pl.when(k % (GB // 2) == GB // 2 - 1)
+        for n in range(len(BACK)):
+
+            @pl.when(k == n + 1)
+            def _():
+                for d in ORDER:
+                    back(n, d).start()
+
+        @pl.when(k % 2 == 1)
         def _():
-            out = k // (GB // 2)
-            for d in ORDER:
-                back(out, d).start()
-            ret[me, pl.ds(pl.multiple_of(out * GB * ML, GB * ML), GB * ML), :] = ana[out, me]
+            own(k // 2).start()
+
+    for n in range(len(BACK)):
+
+        @pl.loop(1, NM)
+        def _(d):
+            back_from(n, d).wait_recv()
 
     @pl.loop(0, BG)
     def _(k):
-        @pl.loop(1, NM)
-        def _(d):
-            back_from(k, d).wait_recv()
-
-    @pl.loop(0, ML)
-    def _(m):
-        for q in range(NM):
-            out_ref[m, q * 8 : q * 8 + 8, :] = ret[q, pl.ds(m, K, stride=ML), :]
+        own(k).wait()
 
     for copy in halos:
         copy.wait_send()
@@ -359,19 +368,23 @@
         def _(k):
             forward(k, d).wait_send()
 
-        @pl.loop(0, BG)
-        def _(k):
-            back(k, d).wait_send()
+        for n in range(len(BACK)):
+            back(n, d).wait_send()
+
+
+def reorder(in_ref, out_ref):
+    for m in range(ML):
+        for q in range(QB):
+            out_ref[m, q * K : q * K + K, :] = in_ref[q, pl.ds(m, K, stride=ML), :]
 
 
 def shards(ensemble, diffusivity, velocity, obs_value, obs_weight, obs_slab, obs_cell):
-    vmem = pl.BlockSpec(memory_space=pltpu.VMEM)
     dma = pltpu.SemaphoreType.DMA
-    return pl.pallas_call(
+    landed = pl.pallas_call(
         kernel,
-        out_shape=jax.ShapeDtypeStruct((ML, NM * K, W), F32),
+        out_shape=jax.ShapeDtypeStruct((NM, K * ML, W), F32),
         in_specs=[pl.BlockSpec(memory_space=pltpu.HBM)] * 7,
-        out_specs=vmem,
+        out_specs=pl.BlockSpec(memory_space=pltpu.HBM),
         scratch_shapes=[
             pltpu.VMEM((ML * ROWS, W), F32),
             pltpu.VMEM((NM * K, W), F32),
@@ -390,7 +403,6 @@
             pltpu.VMEM((ROWS, 2, 8, W), F32),
             pltpu.VMEM((FG, NM, GF, 2, 8, W), F32),
             pltpu.VMEM((BG, NM, GB * ML, W), F32),
-            pltpu.VMEM((NM, K * ML, W), F32),
             pltpu.VMEM((NS, 2 * K, W), F32),
             pltpu.VMEM((NS, 2 * K, W), F32),
             pltpu.VMEM((K, W), F32),
@@ -402,10 +414,11 @@
             dma((2,)),
             dma((FG, NM)),
             dma((FG, NM)),
-            dma((BG, NM)),
-            dma((BG, NM)),
+            dma((len(BACK), NM)),
+            dma((len(BACK), NM)),
             dma((NS,)),
             dma((NS,)),
+            dma((BG,)),
         ],
         compiler_params=pltpu.CompilerParams(
             collective_id=0, has_side_effects=True, vmem_limit_bytes=62 * 2**20
@@ -419,6 +432,14 @@
         obs_slab.reshape(1, OBS),
         obs_cell.reshape(OBS // W, W),
     )
+    return pl.pallas_call(
+        reorder,
+        grid=(NM // QB,),
+        in_specs=[pl.BlockSpec((QB, K * ML, W), lambda i: (i, 0, 0))],
+        out_specs=pl.BlockSpec((ML, QB * K, W), lambda i: (0, i, 0)),
+        out_shape=jax.ShapeDtypeStruct((ML, NM * K, W), F32),
+        compiler_params=pltpu.CompilerParams(vmem_limit_bytes=62 * 2**20),
+    )(landed)
 
 
 def solution(mesh):

time: 115 us -> 113 us (0.983)
  local copies, waits for them, and re-layouts: 2.3 us -> 0 us
    unnamed x1 -> x0, local copies, waits for them, and re-layouts: 2.3 us -> none
    pallas_call x1 -> x2, Pallas kernels: 112 us -> 113 us  [the longest x1 111 us: shards(): pl.pallas_call(kernel, out_shape=jax.ShapeDtypeStruct((NM, K * ML, W), F3...]
where the time goes in v4:
time: 113 us
  Pallas kernels  113 us (100%)
    pallas_call x1, Pallas kernels, shards(): pl.pallas_call(kernel, out_shape=jax.ShapeDtypeStruct((NM, K * ML, W), F3...  111 us

profile of v4, /device:TPU:1, one launch (start us, length us, event | category | flops | bytes accessed | tf_op | source)
XLA Modules:
  0.0 113.0 jit_solution(14420404765057828219)
XLA Ops:
  0.0 110.8 %shard_map.73.in_ref = f32[16,128,128]{2,1,0:T(8,128)} custom-call(f32[2048,128]{1,0:T(8,128)} %bitcast.5, f32[128,128]{1,0:T(8,128)} %dif_hbm.1, f32[2,128,128]{2,1,0:T(8,128)} %vel_hbm.1, f32[10,128]{1,0:T(8,128)} %bitcast.6, f32[10,128]{1,0:T(8,128)} %bitcast.7, s32[1,1280]{1,0:T(1,128)} %bitcast.9, s32[10,128]{1,0:T(8,128)} %bitcast.8), custom_call_target="tpu_custom_call" | custom-call | tf_op jit(solution)/shard_map/pallas_call | solution.py:383
  110.8 2.2 %shard_map.74 = f32[16,128,128]{2,1,0:T(8,128)} custom-call(f32[16,128,128]{2,1,0:T(8,128)} %shard_map.73.in_ref), custom_call_target="tpu_custom_call" | custom-call | tf_op jit(solution)/shard_map/pallas_call | solution.py:435
